TPU v7x, 32 devices: a whole 2x2x4 slice. The times are simulated.
32 devices in a mesh: groups: 2 (over y), row: 4 (over x, core), col: 4 (over z).
Axes of the slice: x: 2, y: 2, z: 4, core: 2. Of those that a mesh axis runs over, the one named last changes fastest.
Arguments:
- features: float32 [32, 65536], P(None, ('groups', 'row', 'col')), parts along dimension 1, may hold values from -6 to 6
- noise: float32 [65536], P(('groups', 'row', 'col')), parts along dimension 0, may hold values from 0.5 to 4
- solution: float32 [16, 65536], P(None, ('groups', 'row', 'col')), parts along dimension 1, may hold values from -6 to 6
- residual: float32 [16, 65536], P(None, ('groups', 'row', 'col')), parts along dimension 1, may hold values from -12 to 12
- direction: float32 [16, 65536], P(None, ('groups', 'row', 'col')), parts along dimension 1, may hold values from -12 to 12
- tile_rows: int32 [8, 4, 64], P(('groups', 'row'), 'col'), parts along dimension 0, may hold values from 0 to 15, as said below
- tile_cols: int32 [8, 4, 64], P(('groups', 'row'), 'col'), parts along dimension 0, may hold values from 0 to 15, as said below
- tile_count: int32 [8, 4], P(('groups', 'row'), 'col'), parts along dimension 0, may hold values from 1 to 64, as said below
Outputs:
- solution_next: float32 [16, 65536], P(None, ('groups', 'row', 'col')), parts along dimension 1
- residual_next: float32 [16, 65536], P(None, ('groups', 'row', 'col')), parts along dimension 1
- direction_next: float32 [16, 65536], P(None, ('groups', 'row', 'col')), parts along dimension 1
There are 2 independent parts, one for each index of `groups`. A program takes and returns all parts, laid end to end along the dimension named above; each array names one. Nothing has to cross between parts.
Inputs may be any that keep to these rules, and one draw needn't show every extreme that they name: `tile_rows`: every listed slot names a tile with I <= J; the slots of one device name distinct tiles. `tile_cols`: see tile_rows. `tile_count`: some device of every problem lists 64 tiles.
All inputs are finite; a program needn't handle non-finite values.
Results may differ from a plain program's by a relative error of at most 0.0003.
Values sent between devices are 32-bit elements; how exact they have to be, the bound alone decides.
A program may use at most 64 MiB of HBM per device.

v0:
```python
import math

import jax
import jax.numpy as jnp
from jax import lax
from jax.sharding import PartitionSpec as P

BLK_DEV = 4


HIGH = lax.Precision.HIGHEST


def tile_kernel(row_points, col_points):
    inner = lax.dot_general(
        row_points,
        col_points,
        (((0,), (0,)), ((), ())),
        precision=HIGH,
        preferred_element_type=jnp.float32,
    )
    row_norms = jnp.sum(row_points * row_points, 0)
    col_norms = jnp.sum(col_points * col_points, 0)
    dist_sq = jnp.maximum(row_norms[:, None] + col_norms[None, :] - 2.0 * inner, 0.0)
    radius = jnp.sqrt(dist_sq) / (1.5 * math.sqrt(row_points.shape[0]))
    inside = jnp.maximum(1.0 - radius, 0.0)
    return inside**4 * (4.0 * radius + 1.0)


def gram(left, right):
    return lax.dot_general(
        left, right, (((1,), (1,)), ((), ())), precision=HIGH, preferred_element_type=jnp.float32
    )


def symmetric(matrix):
    return 0.5 * (matrix + matrix.T)


def spd_solve(matrix, target):
    lower = jnp.linalg.cholesky(matrix)
    half_way = lax.linalg.triangular_solve(lower, target, left_side=True, lower=True)
    return lax.linalg.triangular_solve(
        lower, half_way, left_side=True, lower=True, transpose_a=True
    )


def apply_left(coeffs, field):
    return lax.dot_general(
        coeffs, field, (((0,), (0,)), ((), ())), precision=HIGH, preferred_element_type=jnp.float32
    )


def add_at(running, addend, start):
    axis_last = running.ndim - 1
    current = lax.dynamic_slice_in_dim(running, start, addend.shape[-1], axis_last)
    return lax.dynamic_update_slice_in_dim(running, current + addend, start, axis_last)


def reduce_rows(row_image, row_degree):
    return (
        lax.psum_scatter(row_image, "col", scatter_dimension=1, tiled=True),
        lax.psum_scatter(row_degree, "col", scatter_dimension=0, tiled=True),
    )


def reduce_cols(col_image, col_degree):
    return (
        lax.psum_scatter(col_image, "row", scatter_dimension=1, tiled=True),
        lax.psum_scatter(col_degree, "row", scatter_dimension=0, tiled=True),
    )


def on_device(features, noise, solution, residual, direction, tile_rows, tile_cols, tile_count):
    block_width = features.shape[1] // BLK_DEV
    row_slots = tile_rows[0, 0]
    col_slots = tile_cols[0, 0]
    tile_total = tile_count[0, 0]
    rank_row = lax.axis_index("row")
    rank_col = lax.axis_index("col")
    span = lax.axis_size("col") * BLK_DEV
    row_feat, row_dir = (
        lax.all_gather(features, "col", axis=1, tiled=True),
        lax.all_gather(direction, "col", axis=1, tiled=True),
    )
    col_feat, col_dir = (
        lax.all_gather(features, "row", axis=1, tiled=True),
        lax.all_gather(direction, "row", axis=1, tiled=True),
    )
    side_count = direction.shape[0]
    initial = (
        jnp.zeros((side_count, row_feat.shape[1]), jnp.float32),
        jnp.zeros((row_feat.shape[1],), jnp.float32),
        jnp.zeros((side_count, col_feat.shape[1]), jnp.float32),
        jnp.zeros((col_feat.shape[1],), jnp.float32),
    )

    def one_tile(tile_slot, carried):
        to_row, deg_row, to_col, deg_col = carried
        local_i = row_slots[tile_slot]
        local_j = col_slots[tile_slot]
        start_i = local_i * block_width
        start_j = local_j * block_width
        used_flag = (tile_slot < tile_total).astype(jnp.float32)
        kernel = (
            tile_kernel(
                lax.dynamic_slice_in_dim(row_feat, start_i, block_width, 1),
                lax.dynamic_slice_in_dim(col_feat, start_j, block_width, 1),
            )
            * used_flag
        )
        dir_cols = lax.dynamic_slice_in_dim(col_dir, start_j, block_width, 1)
        row_term = lax.dot_general(
            dir_cols,
            kernel,
            (((1,), (1,)), ((), ())),
            precision=HIGH,
            preferred_element_type=jnp.float32,
        )
        to_row = add_at(to_row, row_term, start_i)
        deg_row = add_at(deg_row, jnp.sum(kernel, 1), start_i)
        big_i = rank_row * span + local_i
        big_j = local_j // BLK_DEV * span + rank_col * BLK_DEV + local_j % BLK_DEV
        mirror = (big_i != big_j).astype(jnp.float32)
        dir_rows = lax.dynamic_slice_in_dim(row_dir, start_i, block_width, 1)
        col_term = (
            lax.dot_general(
                dir_rows,
                kernel,
                (((1,), (0,)), ((), ())),
                precision=HIGH,
                preferred_element_type=jnp.float32,
            )
            * mirror
        )
        to_col = add_at(to_col, col_term, start_j)
        deg_col = add_at(deg_col, jnp.sum(kernel, 0) * mirror, start_j)
        return (to_row, deg_row, to_col, deg_col)

    def one_turn(turn_index, carried):
        for inner_step in range(4):
            carried = one_tile(turn_index * 4 + inner_step, carried)
        return carried

    carried = lax.fori_loop(0, row_slots.shape[0] // 4, one_turn, initial)
    row_image, row_degree = reduce_rows(carried[0], carried[1])
    col_image, col_degree = reduce_cols(carried[2], carried[3])
    degree = row_degree + col_degree
    image = (noise + degree)[None, :] * direction + row_image + col_image
    curv_sum, norm_sum = lax.psum(
        (gram(direction, image), gram(residual, residual)), ("row", "col")
    )
    curvature = symmetric(curv_sum)
    norms_now = symmetric(norm_sum)
    alpha = spd_solve(curvature, norms_now)
    residual_next = residual - apply_left(alpha, image)
    norms_next = symmetric(lax.psum(gram(residual_next, residual_next), ("row", "col")))
    solution_next = solution + apply_left(alpha, direction)
    beta = spd_solve(norms_now, norms_next)
    direction_next = residual_next + apply_left(beta, direction)
    return (solution_next, residual_next, direction_next)


def solution(mesh):
    in_specs = (
        P(None, ("groups", "row", "col")),
        P(("groups", "row", "col")),
        P(None, ("groups", "row", "col")),
        P(None, ("groups", "row", "col")),
        P(None, ("groups", "row", "col")),
        P(("groups", "row"), "col", None),
        P(("groups", "row"), "col", None),
        P(("groups", "row"), "col"),
    )
    out_specs = (
        P(None, ("groups", "row", "col")),
        P(None, ("groups", "row", "col")),
        P(None, ("groups", "row", "col")),
    )
    return jax.shard_map(
        on_device, mesh=mesh, in_specs=in_specs, out_specs=out_specs, check_vma=False
    )
```

profile of v0, /device:TPU:0, one launch (start us, length us, event | category | flops | bytes accessed | tf_op | source)
XLA Modules:
  0.0 874.7 jit_solution(3112990234694962577)
XLA Ops:
  8.8 20.4 %all_gather.15 = f32[16,8192]{1,0:T(8,128)S(1)} all-gather(f32[16,2048]{1,0:T(8,128)S(1)} %copy-done), channel_id=1, replica_groups=mesh['groups'=2,'row'=4,'col'=4] {'col'}, dimensions={1}, use_global_device_ids=true | all-gather | bytes 655360 | tf_op jit(solution)/shard_map/all_gather | solution.py:84
  29.2 7.2 all_gather.12
  36.4 6.0 all-gather.3.cloned.1.call-done
  42.4 17.7 %all-gather.5.cloned.1.call-done = f32[32,8192]{1,0:T(8,128)} async-done(((f32[32,2048]{1,0:T(8,128)}), f32[32,8192]{1,0:T(8,128)}) %all-gather.5.cloned.1.call-update) | async-done | bytes 1048592 | tf_op jit(solution)/shard_map/all_gather | solution.py:87
  60.9 658.3 %while.22 = (s32[]{:T(128)}, f32[16,8192]{1,0:T(8,128)S(1)}, f32[8192]{0:T(1024)S(1)}, f32[16,8192]{1,0:T(8,128)S(1)}, f32[8192]{0:T(1024)S(1)}, /*index=5*/s32[...) while((s32[]{:T(128)}, f32[16,8192]{1,0:T(8,128)S(1)}, ...), condition=%wide.region_17.18_spmd, body=%wide.region_0.17_spmd.sunk | while | flops 821393472 | bytes 14518369 | solution.py:145
  88.2 2.7 fusion.150
  129.4 2.7 fusion.150
  170.5 2.7 fusion.150
  211.6 2.7 fusion.150
  252.7 2.7 fusion.150
  293.9 2.7 fusion.150
  335.1 2.7 fusion.150
  376.3 2.7 fusion.150
  458.5 2.7 fusion.150
  499.6 2.7 fusion.150
  540.8 2.7 fusion.150
  581.9 2.7 fusion.150
  623.1 2.7 fusion.150
  705.3 2.7 fusion.150
  724.0 10.8 %all-reduce.1 = f32[8192]{0:T(1024)S(1)} all-reduce(f32[8192]{0:T(1024)S(1)} %get-tuple-element.410), channel_id=3, replica_groups=mesh['groups'=2,'row'=4,'col'=4] {'row'}, use_global_device_ids=true, to_apply=%region_19.20.clone | all-reduce | flops 8192 | bytes 65536
  734.8 19.6 %all-reduce = f32[8192]{0:T(1024)S(1)} all-reduce(f32[8192]{0:T(1024)S(1)} %get-tuple-element.409), channel_id=2, replica_groups=mesh['groups'=2,'row'=4,'col'=4] {'col'}, use_global_device_ids=true, to_apply=%region_18.19.clone | all-reduce | flops 8192 | bytes 65536
  754.5 9.4 %reduce-scatter.5.cloned.1.call-done = f32[16,2048]{1,0:T(8,128)} async-done(((f32[16,8192]{1,0:T(8,128)}), f32[16,2048]{1,0:T(8,128)}) %reduce-scatter.5.cloned.1.call-update) | async-done | bytes 131088 | tf_op jit(solution)/shard_map/reduce_scatter | solution.py:69
  765.2 60.9 %all-reduce.2 = (f32[16,16]{1,0:T(8,128)S(1)}, f32[16,16]{1,0:T(8,128)S(1)}) all-reduce(f32[16,16]{1,0:T(8,128)S(1)} %fusion.77, f32[16,16]{1,0:T(8,128)S(1)} %convolution_bitcast_fusion), channel_id=1, replica_groups=mesh['groups'=2,'row'=4,'col'=4] {'row','col'}, use_global_device_ids=true, to_apply=%region_25.27 | all-reduce | flops 512 | bytes 4096 | tf_op jit(solution)/shard_map/psum | solution.py:150
  831.3 30.5 %psum.23 = f32[16,16]{1,0:T(8,128)S(1)} all-reduce(f32[16,16]{1,0:T(8,128)S(1)} %fusion.78), channel_id=1, replica_groups=mesh['groups'=2,'row'=4,'col'=4] {'row','col'}, use_global_device_ids=true, to_apply=%region_26.30 | all-reduce | flops 256 | bytes 2048 | tf_op jit(solution)/shard_map/psum | solution.py:157
  (426 shorter events, 313.4 us)
Async XLA Ops:
  7.2 35.2 %all-gather.3.cloned.1.call-start = ((), (), s32[]{:S(2)}) async-start(), calls=%async_computation.2 | async-start | bytes 1310720 | tf_op jit(solution)/shard_map/all_gather | solution.py:83
  7.9 0.9 copy-start
  7.9 52.2 %all-gather.5.cloned.1.call-start = ((), (), s32[]{:S(2)}) async-start(), calls=%async_computation.3 | async-start | bytes 1310720 | tf_op jit(solution)/shard_map/all_gather | solution.py:87
  8.7 745.8 %reduce-scatter.3.cloned.1.call-start = ((), (), s32[]{:S(2)}) async-start(), calls=%async_computation.4 | async-start | bytes 655360 | tf_op jit(solution)/shard_map/reduce_scatter | solution.py:62
  42.4 17.9 %copy-start.4 = (f32[32,8192]{1,0:T(8,128)S(1)}, f32[32,8192]{1,0:T(8,128)}, u32[]{:S(2)}) copy-start(f32[32,8192]{1,0:T(8,128)} %all-gather.3.cloned.1.call-done) | copy-start | bytes 3145732
  60.2 0.7 copy-start.8
  60.2 0.7 copy-start.9
  719.1 0.8 copy-start.2
  719.1 1.0 copy-start.1
  720.0 43.9 %reduce-scatter.5.cloned.1.call-start = ((), (), s32[]{:S(2)}) async-start(), calls=%async_computation.5 | async-start | bytes 655360 | tf_op jit(solution)/shard_map/reduce_scatter | solution.py:69
  720.0 3.7 copy-start.5
  720.5 0.7 copy-start.13
  721.2 0.7 copy-start.12
  734.8 19.6 %copy-start.11 = (f32[2048]{0:T(1024)S(1)}, f32[2048]{0:T(1024)}, u32[]{:S(2)}) copy-start(f32[2048]{0:T(1024)} %param.16) | copy-start | bytes 24580
  763.9 66.8 %copy-start.7 = (f32[16,2048]{1,0:T(8,128)S(1)}, f32[16,2048]{1,0:T(8,128)}, u32[]{:S(2)}) copy-start(f32[16,2048]{1,0:T(8,128)} %reduce-scatter.5.cloned.1.call-done) | copy-start | bytes 393220
  765.2 65.5 %copy-start.6 = (f32[16,2048]{1,0:T(8,128)S(1)}, f32[16,2048]{1,0:T(8,128)}, u32[]{:S(2)}) copy-start(f32[16,2048]{1,0:T(8,128)} %reduce-scatter.3.cloned.1.call-done) | copy-start | bytes 393220
  831.0 35.1 %copy-start.3 = (f32[16,2048]{1,0:T(8,128)}, f32[16,2048]{1,0:T(8,128)S(1)}, u32[]{:S(2)}) copy-start(f32[16,2048]{1,0:T(8,128)S(1)} %convolution_subtract_fusion) | copy-start | bytes 393220
  866.2 1.0 copy-start.10
Sparse Core Ops, SparseCore 0:
  9.6 32.7 all-gather.2
  44.0 16.1 all-gather.4
  720.1 21.4 reduce-scatter.2
  744.0 19.8 reduce-scatter.4
where the time goes:
time: 883 us; the launch traced here: 875 us
  loops' own time  326 us (37%)
  matrix products  276 us (31%)
  blocking collectives  149 us (17%)
  other arithmetic  46.6 us (5%)
  waiting for transfers between devices  35.1 us (4%)
  local copies, waits for them, and re-layouts  25.9 us (3%)
  between operations  15.3 us (2%)
    another operation x1, loops' own time, on_device(): carried = lax.fori_loop(0, row_slots.shape[0] // 4, one_turn, initial)  326 us
    dot_general x64, matrix products, tile_kernel(): lax.dot_general(row_points, col_points, (((0,), (0,)), ((), ())), precisi...  170 us
    dot_general x64, matrix products, one_tile(): lax.dot_general(dir_cols, kernel, (((1,), (1,)), ((), ())), precision=HIG...  61.8 us
    psum x1, blocking collectives, on_device(): lax.psum((gram(direction, image), gram(residual, residual)), ('row', 'col'))  60.9 us
    dot_general x64, matrix products, one_tile(): lax.dot_general(dir_rows, kernel, (((1,), (0,)), ((), ())), precision=HIG...  39.9 us
    psum x1, blocking collectives, on_device(): lax.psum(gram(residual_next, residual_next), ('row', 'col'))  30.5 us
    unnamed x2, blocking collectives  30.4 us
    dynamic_update_slice x128, other arithmetic, add_at(): lax.dynamic_update_slice_in_dim(running, current + addend, start, axis_last)  21.8 us
  transfers between devices with their start and end apart: 4, of which 3 were waited for; matrix products, arithmetic and copies ran while one was open for 0% of the time, Pallas kernels for 0%

commit v1 on v0

v1 whole, which is shorter than its diff:
```python
import functools
import math

import jax
import jax.numpy as jnp
from jax import lax
from jax.experimental import pallas as pl
from jax.experimental.pallas import tpu as pltpu
from jax.sharding import PartitionSpec as P

BLK_DEV = 4
DEPTH = 256
STACK = 48

HIGH = lax.Precision.HIGHEST
BF16 = jnp.bfloat16
F32 = jnp.float32

CUT = 0.25 ** 0.2
TOP = 5.0 * CUT**4
EDGE = 1.0 / CUT


def parts3(x):
    high = x.astype(BF16).astype(F32)
    rest = x - high
    mid = rest.astype(BF16).astype(F32)
    return high, mid, (rest - mid).astype(BF16).astype(F32)


def stack_features(x, left):
    width = x.shape[1]
    norm = jnp.sum(x * x, 0, keepdims=True)
    high, mid, low = parts3(x)
    n_high, n_mid, n_low = parts3(norm)
    ones = jnp.ones((1, width), F32)
    zero = jnp.zeros((2, width), F32)
    if left:
        rows = [high, high, mid, mid, high, low]
        rows += [jnp.concatenate([n_high, n_mid, n_low, ones, ones, ones, zero], 0)]
    else:
        high, mid, low = -2.0 * high, -2.0 * mid, -2.0 * low
        rows = [high, mid, high, mid, low, high]
        rows += [jnp.concatenate([ones, ones, ones, n_high, n_mid, n_low, zero], 0)]
    used = sum(r.shape[0] for r in rows)
    rows += [jnp.zeros((DEPTH - used, width), F32)]
    return jnp.concatenate(rows, 0)


def stack_directions(d):
    high = d.astype(BF16)
    low = (d - high.astype(F32)).astype(BF16)
    return jnp.concatenate([high, low, jnp.ones_like(high)], 0)


def dot(a, b, ca, cb):
    return lax.dot_general(a, b, (((ca,), (cb,)), ((), ())), preferred_element_type=F32)


def tiles_body(
    rows_ref, cols_ref, count_ref, rf_ref, rd_ref, cf_ref, cd_ref,
    to_row, to_col, left, right, d_row, d_col, acc_row, acc_col, *, chunk
):
    n_row, n_col = acc_row.shape[0], acc_col.shape[0]
    side = rd_ref.shape[0]
    width = acc_row.shape[2]
    scale = EDGE / (1.5 * math.sqrt(rf_ref.shape[0]))
    rank_row = lax.axis_index("row")
    rank_col = lax.axis_index("col")
    span = lax.axis_size("col") * BLK_DEV

    def prep_row(b, _):
        at = pl.ds(pl.multiple_of(b * width, width), width)
        left[b] = stack_features(rf_ref[:, at] * scale, True).T.astype(BF16)
        d_row[b] = stack_directions(rd_ref[:, at])
        acc_row[b] = jnp.zeros(acc_row.shape[1:], F32)
        return 0

    def prep_col(b, _):
        at = pl.ds(pl.multiple_of(b * width, width), width)
        right[b] = stack_features(cf_ref[:, at] * scale, False).astype(BF16)
        d_col[b] = stack_directions(cd_ref[:, at])
        acc_col[b] = jnp.zeros(acc_col.shape[1:], F32)
        return 0

    lax.fori_loop(0, n_row, prep_row, 0)
    lax.fori_loop(0, n_col, prep_col, 0)

    def one_tile(t, _):
        i = rows_ref[0, 0, t]
        j = cols_ref[0, 0, t]
        big_i = rank_row * span + i
        big_j = j // BLK_DEV * span + rank_col * BLK_DEV + j % BLK_DEV
        mirror = (big_i != big_j).astype(F32)
        points_j = right[j]
        dirs_j = d_col[j]
        into_col = None
        for c in range(width // chunk):
            at = slice(c * chunk, (c + 1) * chunk)
            dist = jnp.maximum(dot(left[i, at, :], points_j, 1, 0), 1e-30)
            v = jnp.maximum(EDGE - dist * lax.rsqrt(dist), 0.0)
            v2 = v * v
            kern = v2 * v2 * (TOP - v)
            k_high = kern.astype(BF16)
            k_low = (kern - k_high.astype(F32)).astype(BF16)
            acc_row[i, :, at] += dot(dirs_j, k_high, 1, 1) + dot(dirs_j, k_low, 1, 1)
            dirs_i = d_row[i, :, at]
            term = dot(dirs_i, k_high, 1, 0) + dot(dirs_i, k_low, 1, 0)
            into_col = term if into_col is None else into_col + term
        acc_col[j] += into_col * mirror
        return 0

    lax.fori_loop(0, count_ref[0, 0], one_tile, 0)

    def finish(acc, out):
        def one(b, _):
            whole = acc[b]
            out[b, :side] = whole[:side] + whole[side : 2 * side]
            out[b, side:] = whole[2 * side : 2 * side + 8]
            return 0

        lax.fori_loop(0, acc.shape[0], one, 0)

    finish(acc_row, to_row)
    finish(acc_col, to_col)


def tiles_call(rows, cols, count, rf, rd, cf, cd, width):
    n_row, n_col = rf.shape[1] // width, cf.shape[1] // width
    side = rd.shape[0]
    smem = pl.BlockSpec(memory_space=pltpu.SMEM)
    vmem = pl.BlockSpec(memory_space=pltpu.VMEM)
    return pl.pallas_call(
        functools.partial(tiles_body, chunk=256),
        out_shape=(
            jax.ShapeDtypeStruct((n_row, side + 8, width), F32),
            jax.ShapeDtypeStruct((n_col, side + 8, width), F32),
        ),
        in_specs=[smem] * 3 + [vmem] * 4,
        out_specs=(vmem, vmem),
        scratch_shapes=[
            pltpu.VMEM((n_row, width, DEPTH), BF16),
            pltpu.VMEM((n_col, DEPTH, width), BF16),
            pltpu.VMEM((n_row, STACK, width), BF16),
            pltpu.VMEM((n_col, STACK, width), BF16),
            pltpu.VMEM((n_row, STACK, width), F32),
            pltpu.VMEM((n_col, STACK, width), F32),
        ],
        compiler_params=pltpu.CompilerParams(vmem_limit_bytes=60 * 2**20),
        name="tiles",
    )(rows, cols, count, rf, rd, cf, cd)


def gram(left, right):
    return lax.dot_general(
        left, right, (((1,), (1,)), ((), ())), precision=HIGH, preferred_element_type=F32
    )


def symmetric(matrix):
    return 0.5 * (matrix + matrix.T)


def spd_solve(matrix, target):
    lower = jnp.linalg.cholesky(matrix)
    half_way = lax.linalg.triangular_solve(lower, target, left_side=True, lower=True)
    return lax.linalg.triangular_solve(
        lower, half_way, left_side=True, lower=True, transpose_a=True
    )


def apply_left(coeffs, field):
    return lax.dot_general(
        coeffs, field, (((0,), (0,)), ((), ())), precision=HIGH, preferred_element_type=F32
    )


def on_device(features, noise, solution, residual, direction, tile_rows, tile_cols, tile_count):
    width = features.shape[1] // BLK_DEV
    side = direction.shape[0]
    row_feat = lax.all_gather(features, "col", axis=1, tiled=True)
    row_dir = lax.all_gather(direction, "col", axis=1, tiled=True)
    col_feat = lax.all_gather(features, "row", axis=1, tiled=True)
    col_dir = lax.all_gather(direction, "row", axis=1, tiled=True)
    to_row, to_col = tiles_call(
        tile_rows, tile_cols, tile_count, row_feat, row_dir, col_feat, col_dir, width
    )
    mine = lax.psum_scatter(to_row, "col", scatter_dimension=0, tiled=True)
    mine = mine + lax.psum_scatter(to_col, "row", scatter_dimension=0, tiled=True)
    mine = jnp.transpose(mine, (1, 0, 2)).reshape(side + 8, BLK_DEV * width)
    image = (noise + mine[side])[None, :] * direction + mine[:side]
    curv_sum, norm_sum = lax.psum(
        (gram(direction, image), gram(residual, residual)), ("row", "col")
    )
    curvature = symmetric(curv_sum)
    norms_now = symmetric(norm_sum)
    alpha = spd_solve(curvature, norms_now)
    residual_next = residual - apply_left(alpha, image)
    norms_next = symmetric(lax.psum(gram(residual_next, residual_next), ("row", "col")))
    solution_next = solution + apply_left(alpha, direction)
    beta = spd_solve(norms_now, norms_next)
    direction_next = residual_next + apply_left(beta, direction)
    return (solution_next, residual_next, direction_next)


def solution(mesh):
    points = P(None, ("groups", "row", "col"))
    in_specs = (
        points,
        P(("groups", "row", "col")),
        points,
        points,
        points,
        P(("groups", "row"), "col", None),
        P(("groups", "row"), "col", None),
        P(("groups", "row"), "col"),
    )
    return jax.shard_map(
        on_device, mesh=mesh, in_specs=in_specs, out_specs=(points,) * 3, check_vma=False
    )
```

time: 883 us -> 304 us (0.34)
  loops' own time: 326 us -> 0 us
  matrix products: 276 us -> 3.64 us
  waiting for transfers between devices: 35.1 us -> 100 us
  Pallas kernels: 0 us -> 54.8 us
  other arithmetic: 46.6 us -> 9.1 us
  blocking collectives: 149 us -> 120 us
  local copies, waits for them, and re-layouts: 25.9 us -> 1.46 us
    another operation x1 -> x0, loops' own time: 326 us -> none  [on_device(): carried = lax.fori_loop(0, row_slots.shape[0] // 4, one_turn, initial)]
    dot_general x192 -> x0, matrix products: 272 us -> none  [the longest x64 170 us: tile_kernel(): lax.dot_general(row_points, col_points, (((0,), (0,)), ((), ())), precisi...]
    reduce_scatter x2, waiting for transfers between devices: 9.47 us -> 76.2 us  [the longest x1 51.3 us: on_device(): mine = lax.psum_scatter(to_row, 'col', scatter_dimension=0, tiled=True)]
    pallas_call x0 -> x1, Pallas kernels: none -> 54.8 us  [tiles_call(): pl.pallas_call(functools.partial(tiles_body, chunk=256), out_shape=(jax.S...]
    unnamed x2 -> x0, blocking collectives: 30.4 us -> none
    dynamic_slice x32 -> x0, local copies, waits for them, and re-layouts: 22 us -> none  [the longest x16 11 us: one_tile(): local_i = row_slots[tile_slot]]
    dynamic_update_slice x128 -> x0, other arithmetic: 21.8 us -> none  [add_at(): lax.dynamic_update_slice_in_dim(running, current + addend, start, axis_last)]
    reduce_sum x16 -> x0, other arithmetic: 16.7 us -> none  [tile_kernel(): col_norms = jnp.sum(col_points * col_points, 0)]
  transfers between devices with their start and end apart: 4 -> 4, of which waited for: 3 -> 4; matrix products, arithmetic and copies ran while one was open for 0% -> 0% of each run, Pallas kernels for 0% -> 0%
where the time goes in v1:
time: 304 us
  blocking collectives  120 us (39%)
  waiting for transfers between devices  100 us (33%)
  Pallas kernels  54.8 us (18%)
  between operations  14.5 us (5%)
  other arithmetic  9.1 us (3%)
  matrix products  3.64 us (1%)
    psum x1, blocking collectives, on_device(): lax.psum((gram(direction, image), gram(residual, residual)), ('row', 'col'))  60.7 us
    pallas_call x1, Pallas kernels, tiles_call(): pl.pallas_call(functools.partial(tiles_body, chunk=256), out_shape=(jax.S...  54.8 us
    reduce_scatter x1, waiting for transfers between devices, on_device(): mine = lax.psum_scatter(to_row, 'col', scatter_dimension=0, tiled=True)  51.3 us
    psum x1, blocking collectives, on_device(): lax.psum(gram(residual_next, residual_next), ('row', 'col'))  30.4 us
    reduce_scatter x1, waiting for transfers between devices, on_device(): lax.psum_scatter(to_col, 'row', scatter_dimension=0, tiled=True)  24.9 us
    all_gather x1, blocking collectives, on_device(): row_dir = lax.all_gather(direction, 'col', axis=1, tiled=True)  21.6 us
    all_gather x1, waiting for transfers between devices, on_device(): col_feat = lax.all_gather(features, 'row', axis=1, tiled=True)  17.8 us
    all_gather x1, blocking collectives, on_device(): col_dir = lax.all_gather(direction, 'row', axis=1, tiled=True)  7.62 us
  transfers between devices with their start and end apart: 4, of which 4 were waited for; matrix products, arithmetic and copies ran while one was open for 0% of the time, Pallas kernels for 0%

profile of v1, /device:TPU:0, one launch (start us, length us, event | category | flops | bytes accessed | tf_op | source)
XLA Modules:
  0.0 304.4 jit_solution(12832377913027342779)
XLA Ops:
  7.2 0.7 all-gather.3.cloned.1.call-update
  8.0 0.7 all-gather.5.cloned.1.call-update
  9.4 21.6 %all_gather.13.rd_ref = f32[16,8192]{1,0:T(8,128)} all-gather(f32[16,2048]{1,0:T(8,128)S(1)} %copy-done), channel_id=1, replica_groups=mesh['groups'=2,'row'=4,'col'=4] {'col'}, dimensions={1}, use_global_device_ids=true | all-gather | bytes 655360 | tf_op jit(solution)/shard_map/all_gather | solution.py:182
  30.9 7.6 %all_gather.15.cd_ref = f32[16,8192]{1,0:T(8,128)} all-gather(f32[16,2048]{1,0:T(8,128)S(1)} %copy-done), channel_id=1, replica_groups=mesh['groups'=2,'row'=4,'col'=4] {'row'}, dimensions={1}, use_global_device_ids=true | all-gather | bytes 655360 | tf_op jit(solution)/shard_map/all_gather | solution.py:184
  38.5 4.6 %all-gather.3.cloned.1.call-done.rf_ref = f32[32,8192]{1,0:T(8,128)} async-done(((f32[32,2048]{1,0:T(8,128)}), f32[32,8192]{1,0:T(8,128)}) %all-gather.3.cloned.1.call-update) | async-done | bytes 1048592 | tf_op jit(solution)/shard_map/all_gather | solution.py:181
  43.1 17.8 %all-gather.5.cloned.1.call-done.cf_ref = f32[32,8192]{1,0:T(8,128)} async-done(((f32[32,2048]{1,0:T(8,128)}), f32[32,8192]{1,0:T(8,128)}) %all-gather.5.cloned.1.call-update) | async-done | bytes 1048592 | tf_op jit(solution)/shard_map/all_gather | solution.py:183
  60.9 54.8 %tiles.1 = (f32[16,24,512]{2,1,0:T(8,128)}, f32[16,24,512]{2,1,0:T(8,128)}) custom-call(s32[1,1,64]{2,1,0:T(1,128)} %rows_ref.1, s32[1,1,64]{2,1,0:T(1,128)} %cols_ref.1, s32[1,1]{1,0:T(1,128)S(6)} %copy.26.count_ref, f32[32,8192]{1,0:T(8,128)} %all-gather.3.cloned.1.call-done.rf_ref, f32[16,8192]{1,0:T(8,128)} %all_gather.13.rd_ref, ...), custom_call_target="tpu_custom_call" | custom-call | tf_op jit(solution)/shard_map/tiles/pallas_call | solution.py:133
  115.8 0.5 reduce-scatter.5.cloned.1.call-update
  116.9 51.3 %reduce-scatter.3.cloned.1.call-done = f32[4,24,512]{2,1,0:T(8,128)} async-done(((f32[16,24,512]{2,1,0:T(8,128)}), f32[4,24,512]{2,1,0:T(8,128)}) %reduce-scatter.3.cloned.1.call-update) | async-done | bytes 196624 | tf_op jit(solution)/shard_map/reduce_scatter | solution.py:188
  168.2 24.9 %reduce-scatter.5.cloned.1.call-done = f32[4,24,512]{2,1,0:T(8,128)} async-done(((f32[16,24,512]{2,1,0:T(8,128)}), f32[4,24,512]{2,1,0:T(8,128)}) %reduce-scatter.5.cloned.1.call-update) | async-done | bytes 196624 | tf_op jit(solution)/shard_map/reduce_scatter | solution.py:189
  193.1 1.0 add_bitcast_fusion
  194.2 0.7 copy-done.4
  195.2 60.7 %all-reduce = (f32[16,16]{1,0:T(8,128)S(1)}, f32[16,16]{1,0:T(8,128)S(1)}) all-reduce(f32[16,16]{1,0:T(8,128)S(1)} %fusion.20, f32[16,16]{1,0:T(8,128)S(1)} %convolution_bitcast_fusion), channel_id=1, replica_groups=mesh['groups'=2,'row'=4,'col'=4] {'row','col'}, use_global_device_ids=true, to_apply=%region_5.7 | all-reduce | flops 512 | bytes 4096 | tf_op jit(solution)/shard_map/psum | solution.py:192
  256.1 1.5 cholesky.55
  257.6 0.6 compare_reduce_fusion
  258.2 0.6 fusion.3
  258.9 1.2 custom-call.13
  260.2 1.5 cholesky.44
  261.7 0.6 compare_reduce_fusion.1
  262.3 0.6 fusion.2
  263.0 1.2 custom-call.11
  265.1 30.4 %psum.23 = f32[16,16]{1,0:T(8,128)S(1)} all-reduce(f32[16,16]{1,0:T(8,128)S(1)} %fusion.21), channel_id=1, replica_groups=mesh['groups'=2,'row'=4,'col'=4] {'row','col'}, use_global_device_ids=true, to_apply=%region_6.10 | all-reduce | flops 256 | bytes 2048 | tf_op jit(solution)/shard_map/psum | solution.py:199
  296.0 1.0 convolution_add_fusion
  296.9 1.0 convolution_add_fusion.1
  (36 shorter events, 2.7 us)
Async XLA Ops:
  7.2 35.9 %all-gather.3.cloned.1.call-start = ((), (), s32[]{:S(2)}) async-start(), calls=%async_computation.2 | async-start | bytes 1310720 | tf_op jit(solution)/shard_map/all_gather | solution.py:181
  7.9 1.5 copy-start
  7.9 53.0 %all-gather.5.cloned.1.call-start = ((), (), s32[]{:S(2)}) async-start(), calls=%async_computation.3 | async-start | bytes 1310720 | tf_op jit(solution)/shard_map/all_gather | solution.py:183
  8.7 159.5 %reduce-scatter.3.cloned.1.call-start = ((), (), s32[]{:S(2)}) async-start(), calls=%async_computation.4 | async-start | bytes 983040 | tf_op jit(solution)/shard_map/reduce_scatter | solution.py:188
  115.7 77.4 %reduce-scatter.5.cloned.1.call-start = ((), (), s32[]{:S(2)}) async-start(), calls=%async_computation.5 | async-start | bytes 983040 | tf_op jit(solution)/shard_map/reduce_scatter | solution.py:189
  115.8 0.9 copy-start.2
  194.2 0.7 copy-start.4
  264.9 31.1 %copy-start.1 = (f32[16,2048]{1,0:T(8,128)}, f32[16,2048]{1,0:T(8,128)S(1)}, u32[]{:S(2)}) copy-start(f32[16,2048]{1,0:T(8,128)S(1)} %convolution_subtract_fusion) | copy-start | bytes 393220
  295.9 1.0 copy-start.3
Sparse Core Ops, SparseCore 0:
  9.6 33.4 all-gather.2
  44.7 16.1 all-gather.4
  115.8 52.3 reduce-scatter.2
  170.6 22.4 reduce-scatter.4

commit v2 on v1

--- a/solution.py
+++ b/solution.py
@@ -101,11 +101,9 @@
             v = jnp.maximum(EDGE - dist * lax.rsqrt(dist), 0.0)
             v2 = v * v
             kern = v2 * v2 * (TOP - v)
-            k_high = kern.astype(BF16)
-            k_low = (kern - k_high.astype(F32)).astype(BF16)
-            acc_row[i, :, at] += dot(dirs_j, k_high, 1, 1) + dot(dirs_j, k_low, 1, 1)
-            dirs_i = d_row[i, :, at]
-            term = dot(dirs_i, k_high, 1, 0) + dot(dirs_i, k_low, 1, 0)
+            kern = kern.astype(BF16)
+            acc_row[i, :, at] += dot(dirs_j, kern, 1, 1)
+            term = dot(d_row[i, :, at], kern, 1, 0)
             into_col = term if into_col is None else into_col + term
         acc_col[j] += into_col * mirror
         return 0
@@ -113,13 +111,17 @@
     lax.fori_loop(0, count_ref[0, 0], one_tile, 0)
 
     def finish(acc, out):
-        def one(b, _):
-            whole = acc[b]
-            out[b, :side] = whole[:side] + whole[side : 2 * side]
-            out[b, side:] = whole[2 * side : 2 * side + 8]
+        def one(owner, _):
+            degrees = []
+            for b in range(BLK_DEV):
+                whole = acc[owner * BLK_DEV + b]
+                out[owner, b * side : (b + 1) * side] = whole[:side] + whole[side : 2 * side]
+                degrees.append(whole[2 * side : 2 * side + 1])
+            degrees.append(jnp.zeros((8 - BLK_DEV, width), F32))
+            out[owner, BLK_DEV * side :] = jnp.concatenate(degrees, 0)
             return 0
 
-        lax.fori_loop(0, acc.shape[0], one, 0)
+        lax.fori_loop(0, acc.shape[0] // BLK_DEV, one, 0)
 
     finish(acc_row, to_row)
     finish(acc_col, to_col)
@@ -131,10 +133,10 @@
     smem = pl.BlockSpec(memory_space=pltpu.SMEM)
     vmem = pl.BlockSpec(memory_space=pltpu.VMEM)
     return pl.pallas_call(
-        functools.partial(tiles_body, chunk=256),
+        functools.partial(tiles_body, chunk=512),
         out_shape=(
-            jax.ShapeDtypeStruct((n_row, side + 8, width), F32),
-            jax.ShapeDtypeStruct((n_col, side + 8, width), F32),
+            jax.ShapeDtypeStruct((n_row // BLK_DEV, BLK_DEV * side + 8, width), F32),
+            jax.ShapeDtypeStruct((n_col // BLK_DEV, BLK_DEV * side + 8, width), F32),
         ),
         in_specs=[smem] * 3 + [vmem] * 4,
         out_specs=(vmem, vmem),
@@ -151,28 +153,151 @@
     )(rows, cols, count, rf, rd, cf, cd)
 
 
-def gram(left, right):
+def exact_dot(a, b, ca, cb):
     return lax.dot_general(
-        left, right, (((1,), (1,)), ((), ())), precision=HIGH, preferred_element_type=F32
+        a, b, (((ca,), (cb,)), ((), ())), precision=HIGH, preferred_element_type=F32
     )
 
 
-def symmetric(matrix):
-    return 0.5 * (matrix + matrix.T)
-
-
-def spd_solve(matrix, target):
-    lower = jnp.linalg.cholesky(matrix)
-    half_way = lax.linalg.triangular_solve(lower, target, left_side=True, lower=True)
-    return lax.linalg.triangular_solve(
-        lower, half_way, left_side=True, lower=True, transpose_a=True
-    )
-
-
-def apply_left(coeffs, field):
-    return lax.dot_general(
-        coeffs, field, (((0,), (0,)), ((), ())), precision=HIGH, preferred_element_type=F32
-    )
+def invert(matrix):
+    n = matrix.shape[0]
+    rows = lax.broadcasted_iota(jnp.int32, (n, n), 0)
+    cols = lax.broadcasted_iota(jnp.int32, (n, n), 1)
+    both = jnp.concatenate([matrix, (rows == cols).astype(F32)], 1)
+    at = lax.broadcasted_iota(jnp.int32, both.shape, 0)
+    for k in range(n):
+        pivot_row = both[k : k + 1, :] / both[k : k + 1, k : k + 1]
+        both = jnp.where(at == k, pivot_row, both - both[:, k : k + 1] * pivot_row)
+    return both[:, n:]
+
+
+MESH = pl.DeviceIdType.MESH
+
+
+def exchange(name, n, source, landing, send_sem, recv_sem):
+    me = lax.axis_index(name)
+    copies = []
+    for d in range(1, n):
+        owner = lax.rem(me + d, n)
+        copies.append(
+            pltpu.make_async_remote_copy(
+                src_ref=source(owner),
+                dst_ref=landing.at[d - 1],
+                send_sem=send_sem.at[d - 1],
+                recv_sem=recv_sem.at[d - 1],
+                device_id={name: owner},
+                device_id_type=MESH,
+            )
+        )
+        copies[-1].start()
+    return copies
+
+
+def greet(sizes):
+    barrier = pltpu.get_barrier_semaphore()
+    total = 0
+    for name, n in sizes:
+        me = lax.axis_index(name)
+        for d in range(1, n):
+            pl.semaphore_signal(
+                barrier, inc=1, device_id={name: lax.rem(me + d, n)}, device_id_type=MESH
+            )
+        total += n - 1
+    pl.semaphore_wait(barrier, total)
+
+
+def tail_body(
+    to_row, to_col, noise, sol, res, direction, sol_out, res_out, dir_out,
+    land_row, land_col, image, own, land_a, land_b,
+    s_row, r_row, s_col, r_col, s_a, r_a, s_b, r_b, *, n_row, n_col
+):
+    side = direction.shape[0]
+    width = to_row.shape[2]
+    greet((("row", n_row), ("col", n_col)))
+    over_col = exchange("col", n_col, lambda o: to_row.at[o], land_row, s_row, r_row)
+    over_row = exchange("row", n_row, lambda o: to_col.at[o], land_col, s_col, r_col)
+    d = direction[...]
+    r = res[...]
+    gram_res = exact_dot(r, r, 1, 1)
+    for copy in over_row:
+        copy.wait_recv()
+    for copy in over_col:
+        copy.wait_recv()
+    total = to_row[lax.axis_index("col")] + to_col[lax.axis_index("row")]
+    for k in range(n_col - 1):
+        total += land_row[k]
+    for k in range(n_row - 1):
+        total += land_col[k]
+    for b in range(BLK_DEV):
+        at = slice(b * width, (b + 1) * width)
+        shift = noise[:, at] + total[BLK_DEV * side + b : BLK_DEV * side + b + 1]
+        image[:, at] = shift * d[:, at] + total[b * side : (b + 1) * side]
+    im = image[...]
+
+    def all_sum(turn, value):
+        for stage, (name, n, landing, send, recv) in enumerate(
+            (("row", n_row, land_a, s_a, r_a), ("col", n_col, land_b, s_b, r_b))
+        ):
+            mine = own.at[2 * turn + stage]
+            mine[...] = value
+            copies = exchange(
+                name, n, lambda o: mine, landing.at[turn], send.at[turn], recv.at[turn]
+            )
+            for k, copy in enumerate(copies):
+                copy.wait_recv()
+            for k in range(n - 1):
+                value = value + landing[turn, k]
+            waiting.extend(copies)
+        return value
+
+    waiting = over_row + over_col
+    curv = 0.5 * (exact_dot(d, im, 1, 1) + exact_dot(im, d, 1, 1))
+    blank = jnp.zeros((side, 128 - 2 * side), F32)
+    sums = all_sum(0, jnp.concatenate([curv, gram_res, blank], 1))
+    norms = sums[:, side : 2 * side]
+    curv_inv = invert(sums[:, :side])
+    norms_inv = invert(norms)
+    alpha_t = exact_dot(norms, curv_inv, 1, 0)
+    r_next = r - exact_dot(alpha_t, im, 1, 0)
+    res_out[...] = r_next
+    gram_next = exact_dot(r_next, r_next, 1, 1)
+    blank = jnp.zeros((side, 128 - side), F32)
+    sol_out[...] = sol[...] + exact_dot(alpha_t, d, 1, 0)
+    norms_next = all_sum(1, jnp.concatenate([gram_next, blank], 1))[:, :side]
+    beta_t = exact_dot(norms_next, norms_inv, 1, 0)
+    dir_out[...] = r_next + exact_dot(beta_t, d, 1, 0)
+    for copy in waiting:
+        copy.wait_send()
+
+
+def tail_call(to_row, to_col, noise, sol, res, direction):
+    n_col, n_row = to_row.shape[0], to_col.shape[0]
+    side, points = direction.shape
+    vmem = pl.BlockSpec(memory_space=pltpu.VMEM)
+    shape = jax.ShapeDtypeStruct((side, points), F32)
+    dma = pltpu.SemaphoreType.DMA
+    return pl.pallas_call(
+        functools.partial(tail_body, n_row=n_row, n_col=n_col),
+        out_shape=(shape,) * 3,
+        in_specs=[vmem] * 6,
+        out_specs=(vmem,) * 3,
+        scratch_shapes=[
+            pltpu.VMEM((n_col - 1,) + to_row.shape[1:], F32),
+            pltpu.VMEM((n_row - 1,) + to_col.shape[1:], F32),
+            pltpu.VMEM((side, points), F32),
+            pltpu.VMEM((4, side, 128), F32),
+            pltpu.VMEM((2, n_row - 1, side, 128), F32),
+            pltpu.VMEM((2, n_col - 1, side, 128), F32),
+            dma((n_col - 1,)), dma((n_col - 1,)),
+            dma((n_row - 1,)), dma((n_row - 1,)),
+            dma((2, n_row - 1)), dma((2, n_row - 1)),
+            dma((2, n_col - 1)), dma((2, n_col - 1)),
+        ],
+        compiler_params=pltpu.CompilerParams(
+            collective_id=1, has_side_effects=True, vmem_limit_bytes=40 * 2**20
+        ),
+        name="tail",
+    )(to_row, to_col, noise, sol, res, direction)
 
 
 def on_device(features, noise, solution, residual, direction, tile_rows, tile_cols, tile_count):
@@ -185,22 +310,7 @@
     to_row, to_col = tiles_call(
         tile_rows, tile_cols, tile_count, row_feat, row_dir, col_feat, col_dir, width
     )
-    mine = lax.psum_scatter(to_row, "col", scatter_dimension=0, tiled=True)
-    mine = mine + lax.psum_scatter(to_col, "row", scatter_dimension=0, tiled=True)
-    mine = jnp.transpose(mine, (1, 0, 2)).reshape(side + 8, BLK_DEV * width)
-    image = (noise + mine[side])[None, :] * direction + mine[:side]
-    curv_sum, norm_sum = lax.psum(
-        (gram(direction, image), gram(residual, residual)), ("row", "col")
-    )
-    curvature = symmetric(curv_sum)
-    norms_now = symmetric(norm_sum)
-    alpha = spd_solve(curvature, norms_now)
-    residual_next = residual - apply_left(alpha, image)
-    norms_next = symmetric(lax.psum(gram(residual_next, residual_next), ("row", "col")))
-    solution_next = solution + apply_left(alpha, direction)
-    beta = spd_solve(norms_now, norms_next)
-    direction_next = residual_next + apply_left(beta, direction)
-    return (solution_next, residual_next, direction_next)
+    return tail_call(to_row, to_col, noise[None, :], solution, residual, direction)
 
 
 def solution(mesh):

time: 304 us -> 156 us (0.51)
  blocking collectives: 120 us -> 29.2 us
  waiting for transfers between devices: 100 us -> 23.7 us
  Pallas kernels: 54.8 us -> 81.7 us
  other arithmetic: 9.1 us -> 0 us
  matrix products: 3.64 us -> 0 us
    psum x2 -> x0, blocking collectives: 91.1 us -> none  [the longest x1 60.7 us: on_device(): lax.psum((gram(direction, image), gram(residual, residual)), ('row', 'col'))]
    reduce_scatter x2 -> x0, waiting for transfers between devices: 76.2 us -> none  [the longest x1 51.3 us: on_device(): mine = lax.psum_scatter(to_row, 'col', scatter_dimension=0, tiled=True)]
    pallas_call x1 -> x2, Pallas kernels: 54.8 us -> 81.7 us  [the longest x1 68 us: tail_call(): pl.pallas_call(functools.partial(tail_body, n_row=n_row, n_col=n_col), ou...]
    another operation x10 -> x0, other arithmetic: 8.03 us -> none  [the longest x6 4.27 us: spd_solve(): lower = jnp.linalg.cholesky(matrix)]
  transfers between devices with their start and end apart: 4 -> 2, of which waited for: 4 -> 2; matrix products, arithmetic and copies ran while one was open for 0% -> 0% of each run, Pallas kernels for 0% -> 0%
where the time goes in v2:
time: 156 us; the launch traced here: 154 us
  Pallas kernels  81.7 us (52%)
  blocking collectives  29.2 us (19%)
  waiting for transfers between devices  23.7 us (15%)
  between operations  14.7 us (9%)
  local copies, waits for them, and re-layouts  4.1 us (3%)
    pallas_call x1, Pallas kernels, tail_call(): pl.pallas_call(functools.partial(tail_body, n_row=n_row, n_col=n_col), ou...  68 us
    all_gather x1, blocking collectives, on_device(): row_dir = lax.all_gather(direction, 'col', axis=1, tiled=True)  21.6 us
    all_gather x1, waiting for transfers between devices, on_device(): col_feat = lax.all_gather(features, 'row', axis=1, tiled=True)  17.8 us
    pallas_call x1, Pallas kernels, tiles_call(): pl.pallas_call(functools.partial(tiles_body, chunk=512), out_shape=(jax.S...  13.7 us
    all_gather x1, blocking collectives, on_device(): col_dir = lax.all_gather(direction, 'row', axis=1, tiled=True)  7.62 us
    all_gather x1, waiting for transfers between devices, on_device(): row_feat = lax.all_gather(features, 'col', axis=1, tiled=True)  4.56 us
    unnamed x15, local copies, waits for them, and re-layouts  4.1 us
  transfers between devices with their start and end apart: 2, of which 2 were waited for; matrix products, arithmetic and copies ran while one was open for 0% of the time, Pallas kernels for 0%

profile of v2, /device:TPU:0, one launch (start us, length us, event | category | flops | bytes accessed | tf_op | source)
XLA Modules:
  0.0 153.5 jit_solution(15352466834433338983)
XLA Ops:
  7.2 0.0 all-gather.3.cloned.1.call-start
  7.2 0.7 all-gather.3.cloned.1.call-update
  7.9 0.0 copy-start
  7.9 0.0 all-gather.5.cloned.1.call-start
  8.0 0.7 all-gather.5.cloned.1.call-update
  9.3 0.0 copy-done
  9.3 21.6 %all_gather.13.rd_ref = f32[16,8192]{1,0:T(8,128)} all-gather(f32[16,2048]{1,0:T(8,128)S(1)} %copy-done), channel_id=1, replica_groups=mesh['groups'=2,'row'=4,'col'=4] {'col'}, dimensions={1}, use_global_device_ids=true | all-gather | bytes 655360 | tf_op jit(solution)/shard_map/all_gather | solution.py:307
  30.9 7.6 %all_gather.15.cd_ref = f32[16,8192]{1,0:T(8,128)} all-gather(f32[16,2048]{1,0:T(8,128)S(1)} %copy-done), channel_id=1, replica_groups=mesh['groups'=2,'row'=4,'col'=4] {'row'}, dimensions={1}, use_global_device_ids=true | all-gather | bytes 655360 | tf_op jit(solution)/shard_map/all_gather | solution.py:309
  38.5 0.0 copy-start.4
  38.5 4.6 %all-gather.3.cloned.1.call-done.rf_ref = f32[32,8192]{1,0:T(8,128)} async-done(((f32[32,2048]{1,0:T(8,128)}), f32[32,8192]{1,0:T(8,128)}) %all-gather.3.cloned.1.call-update) | async-done | bytes 1048592 | tf_op jit(solution)/shard_map/all_gather | solution.py:306
  43.1 17.8 %all-gather.5.cloned.1.call-done.cf_ref = f32[32,8192]{1,0:T(8,128)} async-done(((f32[32,2048]{1,0:T(8,128)}), f32[32,8192]{1,0:T(8,128)}) %all-gather.5.cloned.1.call-update) | async-done | bytes 1048592 | tf_op jit(solution)/shard_map/all_gather | solution.py:308
  60.8 0.0 copy-start.5
  60.8 13.7 %tiles.1 = (f32[4,72,512]{2,1,0:T(8,128)}, f32[4,72,512]{2,1,0:T(8,128)}) custom-call(s32[1,1,64]{2,1,0:T(1,128)} %rows_ref.1, s32[1,1,64]{2,1,0:T(1,128)} %cols_ref.1, s32[1,1]{1,0:T(1,128)S(6)} %copy.14.count_ref, f32[32,8192]{1,0:T(8,128)} %all-gather.3.cloned.1.call-done.rf_ref, f32[16,8192]{1,0:T(8,128)} %all_gather.13.rd_ref, ...), custom_call_target="tpu_custom_call" | custom-call | tf_op jit(solution)/shard_map/tiles/pallas_call | solution.py:135
  74.5 0.0 copy-done.3
  74.5 0.0 copy-done.4
  74.5 0.0 copy-done.5
  74.5 0.0 copy-start.1
  74.5 1.1 copy-done.1
  75.6 0.0 copy-start.2
  75.6 1.1 copy-done.2
  76.6 68.0 %tail.1 = (f32[16,2048]{1,0:T(8,128)S(1)}, f32[16,2048]{1,0:T(8,128)S(1)}, f32[16,2048]{1,0:T(8,128)S(1)}) custom-call(f32[4,72,512]{2,1,0:T(8,128)S(1)} %copy-done.1, f32[4,72,512]{2,1,0:T(8,128)S(1)} %copy-done.2, f32[1,2048]{1,0:T(1,128)S(1)} %bitcast.1, f32[16,2048]{1,0:T(8,128)S(1)} %copy-done.3, f32[16,2048]{1,0:T(8,128)S(1)} %copy-done.4, ...), custom_call_target="tpu_custom_call" | custom-call | tf_op jit(solution)/shard_map/tail/pallas_call | solution.py:279
  144.7 0.7 copy.15
  145.4 0.7 copy.16
  146.0 0.7 copy.17
  (1 shorter events, 0.0 us)
Async XLA Ops:
  7.2 35.9 %all-gather.3.cloned.1.call-start = ((), (), s32[]{:S(2)}) async-start(), calls=%async_computation | async-start | bytes 1310720 | tf_op jit(solution)/shard_map/all_gather | solution.py:306
  7.9 1.4 copy-start
  7.9 52.9 %all-gather.5.cloned.1.call-start = ((), (), s32[]{:S(2)}) async-start(), calls=%async_computation.1 | async-start | bytes 1310720 | tf_op jit(solution)/shard_map/all_gather | solution.py:308
  38.5 36.0 %copy-start.3 = (f32[16,2048]{1,0:T(8,128)S(1)}, f32[16,2048]{1,0:T(8,128)}, u32[]{:S(2)}) copy-start(f32[16,2048]{1,0:T(8,128)} %sol.1) | copy-start | bytes 393220
  38.5 36.0 %copy-start.4 = (f32[16,2048]{1,0:T(8,128)S(1)}, f32[16,2048]{1,0:T(8,128)}, u32[]{:S(2)}) copy-start(f32[16,2048]{1,0:T(8,128)} %res.1) | copy-start | bytes 393220
  60.8 13.7 %copy-start.5 = (f32[2048]{0:T(1024)S(1)}, f32[2048]{0:T(1024)}, u32[]{:S(2)}) copy-start(f32[2048]{0:T(1024)} %param.9) | copy-start | bytes 24580
  74.5 1.1 copy-start.1
  75.6 1.1 copy-start.2
Sparse Core Ops, SparseCore 0:
  9.6 33.4 all-gather.2
  44.6 16.1 all-gather.4
